TPU v7x, 256 devices: a whole 4x4x8 slice. The times are simulated.
256 devices in a mesh: azi: 8 (over y, core), rad: 16 (over x, z_lo), axl: 2 (over z_hi).
Axes of the slice: x: 4, y: 4, z: 8 (z_hi: 2, z_lo: 4; z = z_hi * 4 + z_lo), core: 2. Of those that a mesh axis runs over, the one named last changes fastest.
Arguments:
- perturbation: float32 [5, 8, 1024, 2048], P(None, 'axl', 'rad', 'azi'), may hold values from -6 to 6
- axial_velocity: float32 [8, 1024], P('axl', 'rad'), may hold values from 0.4 to 1.2
- swirl_velocity: float32 [8, 1024], P('axl', 'rad'), may hold values from -0.8 to 0.8
- sound_speed: float32 [8, 1024], P('axl', 'rad'), may hold values from 1 to 1.6
- rotor_offset: int32 [1], replicated, may hold values from 0 to 2047
Outputs:
- tendency: float32 [5, 8, 1024, 2048], P(None, 'axl', 'rad', 'azi')
All inputs are finite; a program needn't handle non-finite values.
Results may differ from a plain program's by a relative error of at most 0.000065.
Values sent between devices are 32-bit elements; how exact they have to be, the bound alone decides.
No kernel may reach another device: no remote copies, remote signals or barrier semaphores. Data moves between devices by JAX's collectives and lax.ppermute only.
A program may use at most 128 MiB of HBM per device.

v0:
```python
import jax
import jax.numpy as jnp
import numpy as np
from jax import lax
from jax.sharding import PartitionSpec as P

NA = 2048
BAND = 128
WEIGHTS = (45.0 / 60.0, -9.0 / 60.0, 1.0 / 60.0)


def partner(value, axis, distance):
    mask = 2**distance
    pairs = [(source, source ^ mask) for source in range(lax.axis_size(axis))]
    return lax.ppermute(value, axis, pairs)


def with_halo(block, sides, width):
    for axis, dim in sides:
        count = lax.axis_size(axis)
        forward = [(i, i + 1) for i in range(count - 1)]
        backward = [(target, source) for source, target in forward]
        low = lax.ppermute(
            lax.slice_in_dim(block, block.shape[dim] - width, None, axis=dim), axis, forward
        )
        high = lax.ppermute(lax.slice_in_dim(block, 0, width, axis=dim), axis, backward)
        block = jnp.concatenate([low, block, high], axis=dim)
    return block


def stencil_coefs(cells, reach):
    offsets = np.arange(1, reach + 1)
    signs = np.where(offsets % 2 == 1, 1.0, -1.0)
    angles = np.pi * offsets / cells
    values = np.pi / cells * signs * np.cos(angles) / np.sin(angles)
    return np.concatenate([np.zeros(1), values])


def signed_table(coefs, offsets):
    reach = coefs.shape[0] - 1
    magnitude = np.abs(offsets)
    picked = coefs[np.minimum(magnitude, reach)]
    return np.where(magnitude <= reach, np.sign(offsets) * picked, 0.0)


def band_table(coefs, columns):
    reach = coefs.shape[0] - 1
    source = np.arange(columns + 2 * reach)
    target = np.arange(columns)
    offsets = source[:, None] - target[None, :] - reach
    return signed_table(coefs, offsets)


def central_diff(padded, axis_pos):
    extent = padded.shape[axis_pos] - 6
    result = jnp.zeros_like(lax.slice_in_dim(padded, 3, 3 + extent, axis=axis_pos))
    for reach_k, weight in enumerate(WEIGHTS, start=1):
        upper = lax.slice_in_dim(padded, 3 + reach_k, 3 + reach_k + extent, axis=axis_pos)
        lower = lax.slice_in_dim(padded, 3 - reach_k, 3 - reach_k + extent, axis=axis_pos)
        result = result + weight * (upper - lower)
    return result


def section_terms(padded, angular, axial_vel, swirl_vel, sound_vel, metric):
    deriv_x = central_diff(padded, 1)
    stream = axial_vel[:, :, None]
    turning = (swirl_vel * metric[None, :])[:, :, None]
    speed_sq = (sound_vel * sound_vel)[:, :, None]
    scale = metric[:, None]
    convect = stream * deriv_x + turning * angular
    spread = deriv_x[1] + scale * angular[3]
    return jnp.stack(
        [
            -(convect[0] + spread),
            -(convect[1] + deriv_x[4]),
            -convect[2],
            -(convect[3] + scale * angular[4]),
            -(convect[4] + speed_sq * spread),
        ]
    )


def radial_terms(radial, sound_vel):
    speed_sq = (sound_vel * sound_vel)[:, :, None]
    blank = jnp.zeros_like(radial[0])
    return jnp.stack([-radial[0], blank, -radial[1], blank, -speed_sq * radial[0]])


def make_metric(first_row, row_count, radial_total):
    index = (first_row + jnp.arange(row_count, dtype=jnp.int32)).astype(jnp.float32)
    return 2.0 / (1.0 + (index + 0.5) / radial_total)


def rotate_edge(edge_lines, start_cell):
    doubled = jnp.concatenate([edge_lines, edge_lines], axis=3)
    return lax.dynamic_slice_in_dim(doubled, start_cell, NA, 3)


def attach_planes(values, received, stator_side):
    blanks = jnp.zeros_like(received)
    lower = jnp.where(stator_side, blanks, received)
    upper = jnp.where(stator_side, received, blanks)
    return jnp.concatenate([lower, values, upper], axis=1)


def tiled_lines(lines_all, coefs):
    width = BAND
    blocks = NA // width
    lead = lines_all.shape[:3]
    tiles = lines_all.reshape(lead + (blocks, width))
    banded = band_table(coefs, width)
    left_part = jnp.asarray(banded[0:width], dtype=jnp.float32)
    middle_part = jnp.asarray(banded[width : 2 * width], dtype=jnp.float32)
    right_part = jnp.asarray(banded[2 * width : 3 * width], dtype=jnp.float32)
    form = "fxrke,ej->fxrkj"
    middle = jnp.einsum(
        form,
        tiles,
        middle_part,
        precision=lax.Precision.HIGHEST,
        preferred_element_type=jnp.float32,
    )
    from_left = jnp.einsum(
        form, tiles, left_part, precision=lax.Precision.HIGHEST, preferred_element_type=jnp.float32
    )
    from_right = jnp.einsum(
        form, tiles, right_part, precision=lax.Precision.HIGHEST, preferred_element_type=jnp.float32
    )
    result = middle + jnp.roll(from_left, 1, axis=3) + jnp.roll(from_right, -1, axis=3)
    return result.reshape(lines_all.shape)


def per_device(perturbation, axial_velocity, swirl_velocity, sound_speed, rotor_offset):
    azi_count = lax.axis_size("azi")
    rad_count = lax.axis_size("rad")
    rows = perturbation.shape[2]
    sub_rows = rows // azi_count
    azi_pos = lax.axis_index("azi")
    rad_pos = lax.axis_index("rad")
    axl_pos = lax.axis_index("axl")
    radial_total = rows * rad_count
    coefs = stencil_coefs(NA, BAND)
    shift_cells = rotor_offset[0]
    stator_side = axl_pos == 0
    start_cell = jnp.where(stator_side, shift_cells, NA - shift_cells) % NA
    lines_all = lax.all_to_all(perturbation, "azi", split_axis=2, concat_axis=3, tiled=True)
    angular = tiled_lines(lines_all, coefs)
    edge_lines = jnp.where(stator_side, lines_all[:, -3:], lines_all[:, :3])
    received = partner(rotate_edge(edge_lines, start_cell), "axl", 0)
    padded = attach_planes(lines_all, received, stator_side)
    row_start = azi_pos * sub_rows
    axial_sub = lax.dynamic_slice_in_dim(axial_velocity, row_start, sub_rows, 1)
    swirl_sub = lax.dynamic_slice_in_dim(swirl_velocity, row_start, sub_rows, 1)
    sound_sub = lax.dynamic_slice_in_dim(sound_speed, row_start, sub_rows, 1)
    metric = make_metric(rad_pos * rows + row_start, sub_rows, radial_total)
    partial_lines = section_terms(padded, angular, axial_sub, swirl_sub, sound_sub, metric)
    partial_value = lax.all_to_all(partial_lines, "azi", split_axis=3, concat_axis=2, tiled=True)
    pair = jnp.stack([perturbation[2], perturbation[4]])
    pair_pad = with_halo(pair, (("rad", 2),), 3)
    radial = central_diff(pair_pad, 2)
    return partial_value + radial_terms(radial, sound_speed)


def solution(mesh):
    return jax.shard_map(
        per_device,
        mesh=mesh,
        in_specs=(
            P(None, "axl", "rad", "azi"),
            P("axl", "rad"),
            P("axl", "rad"),
            P("axl", "rad"),
            P(),
        ),
        out_specs=P(None, "axl", "rad", "azi"),
        check_vma=False,
    )
```

profile of v0, /device:TPU:1, one launch (start us, length us, event | category | flops | bytes accessed | tf_op | source)
XLA Modules:
  0.0 211.9 jit_solution(11327305505855242520)
XLA Ops:
  0.0 3.5 %copy.17 = f32[5,4,64,256]{3,0,1,2:T(8,128)} copy(f32[5,4,64,256]{3,2,1,0:T(8,128)} %param.8) | data formatting | bytes 2621440 | tf_op args[0]
  3.5 6.7 %all-to-all-start = ((f32[5,4,64,256]{3,0,1,2:T(8,128)}), f32[5,4,64,256]{3,0,1,2:T(8,128)S(1)}, u32[]{:S(2)}, u32[]{:S(2)}) async-start(f32[5,4,64,256]{3,0,1,2:T(8,128)} %copy.17), calls=%async_computation | async-start | bytes 4194304 | tf_op jit(solution)/shard_map/all_to_all | solution.py:146
  10.2 1.1 fusion.32
  11.4 1.3 collective-permute-start.1
  12.7 4.0 %collective-permute-start.2 = (f32[2,4,3,256]{3,2,1,0:T(4,128)S(1)}, f32[2,4,3,256]{3,2,1,0:T(4,128)S(1)}, u32[]{:S(2)}, u32[]{:S(2)}) collective-permute-start(f32[2,4,3,256]{3,2,1,0:T(4,128)S(1)} %get-tuple-element.16), channel_id=1, source_target_pairs={{0,2},{2,4},{4,6},{6,8},{8,10},{10,12},{12,14},{14,16},{16,18},{18... | collective-permute-start | bytes 73736 | tf_op jit(solution)/shard_map/ppermute | solution.py:23
  17.7 0.9 pad_maximum_fusion.2
  18.6 18.0 %all-to-all-done = f32[5,4,64,256]{3,0,1,2:T(8,128)S(1)} async-done(((f32[5,4,64,256]{3,0,1,2:T(8,128)}), f32[5,4,64,256]{3,0,1,2:T(8,128)S(1)}, u32[]{:S(2)}, u32[]{:S(2)}) %all-to-all-start) | async-done | bytes 1310752 | tf_op jit(solution)/shard_map/all_to_all | solution.py:146
  36.6 1.3 copy-done.1
  37.9 2.4 %copy.25 = f32[5,4,8,8,256]{4,2,3,1,0:T(8,128)S(1)} copy(f32[5,4,8,8,256]{4,0,1,3,2:T(8,128)} %bitcast.54) | data formatting | bytes 2621440 | tf_op jit(solution)/shard_map/all_to_all | solution.py:146
  40.3 1.0 copy-done
  41.5 1.4 reshape.55
  43.0 1.6 fusion.14
  44.5 6.1 %collective-permute-start = (f32[5,3,8,2048]{3,2,1,0:T(8,128)}, f32[5,3,8,2048]{3,2,1,0:T(8,128)}, u32[]{:S(2)}, u32[]{:S(2)}) collective-permute-start(f32[5,3,8,2048]{3,2,1,0:T(8,128)} %fusion.14), channel_id=1, source_target_pairs={{0,1},{1,0},{2,3},{3,2},{4,5},{5,4},{6,7},{7,6},{8,9},{9,8},{10,11... | collective-permute-start | bytes 2949128 | tf_op jit(solution)/shard_map/ppermute | solution.py:15
  50.7 1.2 convolution_bitcast_fusion
  52.7 1.2 convolution_bitcast_fusion.1
  54.0 2.5 %fusion.1 = f32[5,4,8,16,128]{4,3,2,1,0:T(8,128)} fusion(f32[128,128,1,1,1]{1,0,4,3,2:T(8,128)S(1)} %copy-done.4, f32[5,4,8,16,128]{4,3,2,1,0:T(8,128)S(1)} %reshape.55, f32[5,4,8,15,128]{4,3,2,1,0:T(8,128)S(1)} %bitcast.55, f32[5,4,8,1,128]{4,3,2,1,0:T(1,128)S(1)} %slice.161, f32[5,4,8,1,128]{4,3,2,1,0:T(1,128)S(1)} %slice.164, ...), kind=kOutput, calls=%fused_computation.14 | convolution fusion | flops 504627200 | bytes 5308416 | tf_op jit(solution)/shard_map/fxrke,ej->fxrkj/dot_general | solution.py:116
  56.5 1.5 reshape.56
  58.0 1.9 fusion.31
  59.9 1.0 squeeze.7
  60.9 1.7 squeeze.8
  62.6 14.3 %collective-permute-done = f32[5,3,8,2048]{3,2,1,0:T(8,128)} collective-permute-done((f32[5,3,8,2048]{3,2,1,0:T(8,128)}, f32[5,3,8,2048]{3,2,1,0:T(8,128)}, u32[]{:S(2)}, u32[]{:S(2)}) %collective-permute-start) | collective-permute-done | bytes 983072 | tf_op jit(solution)/shard_map/ppermute | solution.py:15
  76.9 1.4 broadcast_select_fusion.1
  78.3 1.1 multiply_add_fusion
  80.6 12.5 %copy.19 = f32[5,4,8,2048]{2,1,0,3:T(4,128)} copy(f32[5,4,8,2048]{3,2,1,0:T(8,128)S(1)} %fusion.22) | data formatting | bytes 2621440 | tf_op jit(solution)/shard_map/stack | solution.py:72
  93.1 26.6 %reshape.60 = f32[8,1,40960]{2,1,0:T(1,128)} reshape(f32[2048,5,4,8]{3,2,1,0:T(4,128)} %bitcast.50) | data formatting | bytes 2621440
  119.8 20.2 %all-to-all-start.1 = ((f32[8,1,40960]{2,1,0:T(1,128)}), f32[8,1,40960]{2,1,0:T(1,128)S(1)}, u32[]{:S(2)}, u32[]{:S(2)}) async-start(f32[8,1,40960]{2,1,0:T(1,128)} %reshape.60), calls=%async_computation.1 | async-start | bytes 2621440 | tf_op jit(solution)/shard_map/all_to_all | solution.py:157
  143.2 0.8 multiply_dynamic-update-slice_fusion
  144.0 13.9 %all-to-all-done.1 = f32[8,1,40960]{2,1,0:T(1,128)S(1)} async-done(((f32[8,1,40960]{2,1,0:T(1,128)}), f32[8,1,40960]{2,1,0:T(1,128)S(1)}, u32[]{:S(2)}, u32[]{:S(2)}) %all-to-all-start.1) | async-done | bytes 1310752 | tf_op jit(solution)/shard_map/all_to_all | solution.py:157
  158.4 3.7 %reduce = f32[8,40960]{1,0:T(8,128)S(1)} reduce(f32[8,1,40960]{2,1,0:T(1,128)S(1)} %all-to-all-done.1, f32[]{:T(128)} %broadcast.89), dimensions={1}, to_apply=%all_to_all.30.reduce_sub_computation | reduce | bytes 2621444 | tf_op jit(solution)/shard_map/all_to_all | solution.py:157
  162.2 32.6 %reshape.61 = f32[2048,5,4,8]{3,2,1,0:T(4,128)} reshape(f32[8,40960]{1,0:T(8,128)S(1)} %reduce) | data formatting | bytes 2621440
  194.8 14.5 %copy.20 = f32[5,4,8,8,256]{4,3,2,1,0:T(8,128)S(1)} copy(f32[5,4,8,8,256]{3,1,0,4,2:T(4,128)} %bitcast.51) | data formatting | bytes 2621440 | tf_op jit(solution)/shard_map/all_to_all | solution.py:157
  209.4 2.6 %bitcast_add_fusion = f32[5,4,64,256]{3,2,1,0:T(8,128)} fusion(f32[5,4,64,256]{3,2,1,0:T(8,128)} %multiply_dynamic-update-slice_fusion, f32[5,4,8,8,256]{4,3,2,1,0:T(8,128)S(1)} %copy.20), kind=kLoop, calls=%fused_computation.29 | loop fusion | flops 327680 | bytes 3932160 | tf_op jit(solution)/shard_map/add | solution.py:161
  (41 shorter events, 6.4 us)
Async XLA Ops:
  3.5 33.1 %all-to-all-start = ((f32[5,4,64,256]{3,0,1,2:T(8,128)}), f32[5,4,64,256]{3,0,1,2:T(8,128)S(1)}, u32[]{:S(2)}, u32[]{:S(2)}) async-start(f32[5,4,64,256]{3,0,1,2:T(8,128)} %copy.17), calls=%async_computation | async-start | bytes 4194304 | tf_op jit(solution)/shard_map/all_to_all | solution.py:146
  10.2 6.5 %copy-start.7 = (f32[4,64]{1,0:T(4,128)S(1)}, f32[4,64]{1,0:T(4,128)}, u32[]{:S(2)}) copy-start(f32[4,64]{1,0:T(4,128)} %param.11) | copy-start | bytes 3076
  10.2 6.5 %copy-start.8 = (f32[4,64]{1,0:T(4,128)S(1)}, f32[4,64]{1,0:T(4,128)}, u32[]{:S(2)}) copy-start(f32[4,64]{1,0:T(4,128)} %param.10) | copy-start | bytes 3076
  10.2 6.5 %copy-start.9 = (f32[4,64]{1,0:T(4,128)S(1)}, f32[4,64]{1,0:T(4,128)}, u32[]{:S(2)}) copy-start(f32[4,64]{1,0:T(4,128)} %param.9) | copy-start | bytes 3076
  11.4 6.2 %collective-permute-start.1 = (f32[2,4,3,256]{3,2,1,0:T(4,128)S(1)}, f32[2,4,3,256]{3,2,1,0:T(4,128)S(1)}, u32[]{:S(2)}, u32[]{:S(2)}) collective-permute-start(f32[2,4,3,256]{3,2,1,0:T(4,128)S(1)} %get-tuple-element.15), channel_id=1, source_target_pairs={{2,0},{4,2},{6,4},{8,6},{10,8},{12,10},{14,12},{16,14},{18,16},{20... | collective-permute-start | bytes 73736 | tf_op jit(solution)/shard_map/ppermute | solution.py:26
  12.7 5.0 %collective-permute-start.2 = (f32[2,4,3,256]{3,2,1,0:T(4,128)S(1)}, f32[2,4,3,256]{3,2,1,0:T(4,128)S(1)}, u32[]{:S(2)}, u32[]{:S(2)}) collective-permute-start(f32[2,4,3,256]{3,2,1,0:T(4,128)S(1)} %get-tuple-element.16), channel_id=1, source_target_pairs={{0,2},{2,4},{4,6},{6,8},{8,10},{10,12},{12,14},{14,16},{16,18},{18... | collective-permute-start | bytes 73736 | tf_op jit(solution)/shard_map/ppermute | solution.py:23
  36.6 1.3 copy-start.1
  40.2 1.1 copy-start
  43.0 7.7 %copy-start.6 = (f32[128,128,1,1,1]{1,0,4,3,2:T(8,128)S(1)}, f32[128,128,1,1,1]{1,0,4,3,2:T(8,128)}, u32[]{:S(2)}) copy-start(f32[128,128,1,1,1]{1,0,4,3,2:T(8,128)} %constant.66) | copy-start | bytes 196612
  44.5 32.3 %collective-permute-start = (f32[5,3,8,2048]{3,2,1,0:T(8,128)}, f32[5,3,8,2048]{3,2,1,0:T(8,128)}, u32[]{:S(2)}, u32[]{:S(2)}) collective-permute-start(f32[5,3,8,2048]{3,2,1,0:T(8,128)} %fusion.14), channel_id=1, source_target_pairs={{0,1},{1,0},{2,3},{3,2},{4,5},{5,4},{6,7},{7,6},{8,9},{9,8},{10,11... | collective-permute-start | bytes 2949128 | tf_op jit(solution)/shard_map/ppermute | solution.py:15
  51.8 0.8 copy-start.5
  52.7 1.3 copy-start.4
  79.4 1.0 copy-start.3
  119.8 20.2 %copy-start.2 = (f32[2,4,67,256]{3,2,1,0:T(8,128)S(1)}, f32[2,4,67,256]{3,2,1,0:T(8,128)}, u32[]{:S(2)}) copy-start(f32[2,4,67,256]{3,2,1,0:T(8,128)} %get-tuple-element.14) | copy-start | bytes 1646596
  119.8 38.1 %all-to-all-start.1 = ((f32[8,1,40960]{2,1,0:T(1,128)}), f32[8,1,40960]{2,1,0:T(1,128)S(1)}, u32[]{:S(2)}, u32[]{:S(2)}) async-start(f32[8,1,40960]{2,1,0:T(1,128)} %reshape.60), calls=%async_computation.1 | async-start | bytes 2621440 | tf_op jit(solution)/shard_map/all_to_all | solution.py:157
where the time goes:
time: 213 us; the launch traced here: 212 us
  local copies, waits for them, and re-layouts  107 us (50%)
  waiting for transfers between devices  46.3 us (22%)
  starting transfers between devices  38.4 us (18%)
  other arithmetic  14.5 us (7%)
  matrix products  4.92 us (2%)
    unnamed x25, local copies, waits for them, and re-layouts  68 us
    all_to_all x1, starting transfers between devices, per_device(): lax.all_to_all(partial_lines, 'azi', split_axis=3, concat_axis=2, tiled=T...  20.2 us
    all_to_all x1, waiting for transfers between devices, per_device(): lax.all_to_all(perturbation, 'azi', split_axis=2, concat_axis=3, tiled=True)  18 us
    all_to_all x2, local copies, waits for them, and re-layouts, per_device(): lax.all_to_all(partial_lines, 'azi', split_axis=3, concat_axis=2, tiled=T...  15.1 us
    ppermute x1, waiting for transfers between devices, partner(): return lax.ppermute(value, axis, pairs)  14.3 us
    all_to_all x1, waiting for transfers between devices, per_device(): lax.all_to_all(partial_lines, 'azi', split_axis=3, concat_axis=2, tiled=T...  13.9 us
    another operation x1, local copies, waits for them, and re-layouts, section_terms(): jnp.stack([-(convect[0] + spread), -(convect[1] + deriv_x[4]), -convect[2...  12.5 us
    all_to_all x1, starting transfers between devices, per_device(): lax.all_to_all(perturbation, 'azi', split_axis=2, concat_axis=3, tiled=True)  6.74 us
  transfers between devices with their start and end apart: 5, of which 4 were waited for; matrix products, arithmetic and copies ran while one was open for 8% of the time, Pallas kernels for 0%

commit v1 on v0

--- a/solution.py
+++ b/solution.py
@@ -7,6 +7,28 @@
 NA = 2048
 BAND = 128
 WEIGHTS = (45.0 / 60.0, -9.0 / 60.0, 1.0 / 60.0)
+
+
+def cut_along(value, dim, peers):
+    before, after = (value.shape[:dim], value.shape[dim + 1 :])
+    return jnp.moveaxis(value.reshape(*before, peers, -1, *after), dim, 0)
+
+
+def laid_out(blocks, dim):
+    blocks = jnp.moveaxis(blocks, 0, dim)
+    dims = blocks.shape
+    return blocks.reshape(*dims[:dim], dims[dim] * dims[dim + 1], *dims[dim + 2 :])
+
+
+def swapped_with_each(array, axis, split_dim, concat_dim):
+    size, index = (lax.axis_size(axis), lax.axis_index(axis))
+    tiles = cut_along(array, split_dim, size)
+    done = [tiles[index]]
+    for step in range(1, size):
+        sent = tiles[index ^ step]
+        done.append(lax.ppermute(sent, axis, [(i, i ^ step) for i in range(size)]))
+    tiles = jnp.stack(done)[index ^ jnp.arange(size)]
+    return laid_out(tiles, concat_dim)
 
 
 def partner(value, axis, distance):
@@ -154,7 +176,7 @@
     sound_sub = lax.dynamic_slice_in_dim(sound_speed, row_start, sub_rows, 1)
     metric = make_metric(rad_pos * rows + row_start, sub_rows, radial_total)
     partial_lines = section_terms(padded, angular, axial_sub, swirl_sub, sound_sub, metric)
-    partial_value = lax.all_to_all(partial_lines, "azi", split_axis=3, concat_axis=2, tiled=True)
+    partial_value = swapped_with_each(partial_lines, "azi", 3, 2)
     pair = jnp.stack([perturbation[2], perturbation[4]])
     pair_pad = with_halo(pair, (("rad", 2),), 3)
     radial = central_diff(pair_pad, 2)

time: 213 us -> 128 us (0.60)
  local copies, waits for them, and re-layouts: 107 us -> 12.8 us
  waiting for transfers between devices: 46.3 us -> 53.5 us
  starting transfers between devices: 38.4 us -> 44.3 us
  other arithmetic: 14.5 us -> 9.85 us
    unnamed x25 -> x34, local copies, waits for them, and re-layouts: 68 us -> 5.57 us
    ppermute x0 -> x7, starting transfers between devices: none -> 25.5 us  [swapped_with_each(): done.append(lax.ppermute(sent, axis, [(i, i ^ step) for i in range(size)]))]
    all_to_all x1 -> x0, starting transfers between devices: 20.2 us -> none  [per_device(): lax.all_to_all(partial_lines, 'azi', split_axis=3, concat_axis=2, tiled=T...]
    all_to_all x2 -> x0, local copies, waits for them, and re-layouts: 15.1 us -> none  [per_device(): lax.all_to_all(partial_lines, 'azi', split_axis=3, concat_axis=2, tiled=T...]
    all_to_all x1 -> x0, waiting for transfers between devices: 13.9 us -> none  [per_device(): lax.all_to_all(partial_lines, 'azi', split_axis=3, concat_axis=2, tiled=T...]
    ppermute x0 -> x7, waiting for transfers between devices: none -> 13.9 us  [swapped_with_each(): done.append(lax.ppermute(sent, axis, [(i, i ^ step) for i in range(size)]))]
    another operation x1, local copies, waits for them, and re-layouts: 12.5 us -> 0.02 us  [section_terms(): jnp.stack([-(convect[0] + spread), -(convect[1] + deriv_x[4]), -convect[2...]
    all_to_all x1, waiting for transfers between devices: 18 us -> 22 us  [per_device(): lax.all_to_all(perturbation, 'azi', split_axis=2, concat_axis=3, tiled=True)]
  transfers between devices with their start and end apart: 5 -> 11, of which waited for: 4 -> 7; matrix products, arithmetic and copies ran while one was open for 8% -> 11% of each run, Pallas kernels for 0% -> 0%
where the time goes in v1:
time: 128 us; the launch traced here: 126 us
  waiting for transfers between devices  53.5 us (42%)
  starting transfers between devices  44.3 us (35%)
  local copies, waits for them, and re-layouts  12.8 us (10%)
  other arithmetic  9.85 us (8%)
  matrix products  4.95 us (4%)
    ppermute x7, starting transfers between devices, swapped_with_each(): done.append(lax.ppermute(sent, axis, [(i, i ^ step) for i in range(size)]))  25.5 us
    all_to_all x1, waiting for transfers between devices, per_device(): lax.all_to_all(perturbation, 'azi', split_axis=2, concat_axis=3, tiled=True)  22 us
    ppermute x1, waiting for transfers between devices, partner(): return lax.ppermute(value, axis, pairs)  17.6 us
    ppermute x7, waiting for transfers between devices, swapped_with_each(): done.append(lax.ppermute(sent, axis, [(i, i ^ step) for i in range(size)]))  13.9 us
    all_to_all x1, starting transfers between devices, per_device(): lax.all_to_all(perturbation, 'azi', split_axis=2, concat_axis=3, tiled=True)  6.42 us
    ppermute x1, starting transfers between devices, partner(): return lax.ppermute(value, axis, pairs)  6.12 us
    unnamed x34, local copies, waits for them, and re-layouts  5.57 us
    ppermute x1, starting transfers between devices, with_halo(): lax.ppermute(lax.slice_in_dim(block, block.shape[dim] - width, None, axis...  5 us
  transfers between devices with their start and end apart: 11, of which 7 were waited for; matrix products, arithmetic and copies ran while one was open for 11% of the time, Pallas kernels for 0%

profile of v1, /device:TPU:1, one launch (start us, length us, event | category | flops | bytes accessed | tf_op | source)
XLA Modules:
  0.0 126.5 jit_solution(8952857609758073742)
XLA Ops:
  0.0 1.2 fusion.30
  1.2 1.3 %collective-permute-start.8 = (f32[2,4,3,256]{3,2,1,0:T(4,128)S(1)}, f32[2,4,3,256]{3,2,1,0:T(4,128)S(1)}, u32[]{:S(2)}, u32[]{:S(2)}) collective-permute-start(f32[2,4,3,256]{3,2,1,0:T(4,128)S(1)} %get-tuple-element.27), channel_id=1, source_target_pairs={{2,0},{4,2},{6,4},{8,6},{10,8},{12,10},{14,12},{16,14},{18,16},{20... | collective-permute-start | bytes 73736 | tf_op jit(solution)/shard_map/ppermute | solution.py:48
  2.5 5.0 %collective-permute-start.9 = (f32[2,4,3,256]{3,2,1,0:T(4,128)S(1)}, f32[2,4,3,256]{3,2,1,0:T(4,128)S(1)}, u32[]{:S(2)}, u32[]{:S(2)}) collective-permute-start(f32[2,4,3,256]{3,2,1,0:T(4,128)S(1)} %get-tuple-element.28), channel_id=1, source_target_pairs={{0,2},{2,4},{4,6},{6,8},{8,10},{10,12},{12,14},{14,16},{16,18},{18... | collective-permute-start | bytes 73736 | tf_op jit(solution)/shard_map/ppermute | solution.py:45
  7.5 2.2 %copy.31 = f32[5,4,64,256]{3,0,1,2:T(8,128)} copy(f32[5,4,64,256]{3,2,1,0:T(8,128)S(1)} %copy-done.3) | data formatting | bytes 2621440 | tf_op args[0]
  9.7 6.4 %all-to-all-start = ((f32[5,4,64,256]{3,0,1,2:T(8,128)}), f32[5,4,64,256]{3,0,1,2:T(8,128)S(1)}, u32[]{:S(2)}, u32[]{:S(2)}) async-start(f32[5,4,64,256]{3,0,1,2:T(8,128)} %copy.31), calls=%async_computation | async-start | bytes 4194304 | tf_op jit(solution)/shard_map/all_to_all | solution.py:168
  17.5 0.8 negate_dynamic-update-slice_fusion
  20.5 22.0 %all-to-all-done = f32[5,4,64,256]{3,0,1,2:T(8,128)S(1)} async-done(((f32[5,4,64,256]{3,0,1,2:T(8,128)}), f32[5,4,64,256]{3,0,1,2:T(8,128)S(1)}, u32[]{:S(2)}, u32[]{:S(2)}) %all-to-all-start) | async-done | bytes 1310752 | tf_op jit(solution)/shard_map/all_to_all | solution.py:168
  42.5 0.8 copy.53
  43.2 1.1 copy-done
  44.4 1.5 %all_to_all.16 = f32[5,4,8,2048]{3,2,1,0:T(8,128)S(1)} reshape(f32[5,4,8,8,256]{4,3,2,1,0:T(8,128)} %bitcast.102) | data formatting | bytes 2621440 | tf_op jit(solution)/shard_map/all_to_all | solution.py:168
  46.0 1.5 %fusion.14 = f32[5,3,8,2048]{3,2,1,0:T(8,128)} fusion(s32[]{:T(128)S(6)} %select_n.73, f32[5,3,8,2048]{3,2,1,0:T(8,128)S(1)} %slice_select_fusion), kind=kLoop, calls=%fused_computation.33 | loop fusion | flops 245760 | bytes 1966084 | tf_op jit(solution)/shard_map/concatenate | solution.py:117
  47.6 6.1 %collective-permute-start = (f32[5,3,8,2048]{3,2,1,0:T(8,128)}, f32[5,3,8,2048]{3,2,1,0:T(8,128)}, u32[]{:S(2)}, u32[]{:S(2)}) collective-permute-start(f32[5,3,8,2048]{3,2,1,0:T(8,128)} %fusion.14), channel_id=1, source_target_pairs={{0,1},{1,0},{2,3},{3,2},{4,5},{5,4},{6,7},{7,6},{8,9},{9,8},{10,11... | collective-permute-start | bytes 2949128 | tf_op jit(solution)/shard_map/ppermute | solution.py:37
  53.7 1.2 convolution_bitcast_fusion
  55.8 1.2 convolution_bitcast_fusion.1
  57.1 2.6 %fusion.1 = f32[5,4,8,16,128]{4,3,2,1,0:T(8,128)} fusion(f32[128,128,1,1,1]{1,0,4,3,2:T(8,128)S(1)} %copy-done.4, f32[5,4,8,16,128]{4,3,2,1,0:T(8,128)S(1)} %reshape.95, f32[5,4,8,15,128]{4,3,2,1,0:T(8,128)S(1)} %bitcast.104, f32[5,4,8,1,128]{4,3,2,1,0:T(1,128)S(1)} %slice.163, f32[5,4,8,1,128]{4,3,2,1,0:T(1,128)S(1)} %slice.166, ...), kind=kOutput, calls=%fused_computation.15 | convolution fusion | flops 504627200 | bytes 5308416 | tf_op jit(solution)/shard_map/fxrke,ej->fxrkj/dot_general | solution.py:138
  59.6 1.5 %reshape.96 = f32[5,4,8,2048]{3,2,1,0:T(8,128)S(1)} reshape(f32[5,4,8,16,128]{4,3,2,1,0:T(8,128)} %fusion.1) | data formatting | bytes 2621440 | tf_op jit(solution)/shard_map/reshape | solution.py:152
  61.1 1.1 fusion.29
  62.3 17.6 %collective-permute-done = f32[5,3,8,2048]{3,2,1,0:T(8,128)} collective-permute-done((f32[5,3,8,2048]{3,2,1,0:T(8,128)}, f32[5,3,8,2048]{3,2,1,0:T(8,128)}, u32[]{:S(2)}, u32[]{:S(2)}) %collective-permute-start) | collective-permute-done | bytes 983072 | tf_op jit(solution)/shard_map/ppermute | solution.py:37
  79.9 1.4 %broadcast_select_fusion.1 = (f32[5,3,8,2048]{3,2,1,0:T(8,128)S(1)}, f32[5,3,8,2048]{3,2,1,0:T(8,128)S(1)}) fusion(f32[5,3,8,2048]{3,2,1,0:T(8,128)} %collective-permute-done, pred[]{:T(512)S(6)} %eq.5), kind=kLoop, calls=%fused_computation.46 | loop fusion | flops 491520 | bytes 2949121 | tf_op jit(solution)/shard_map/jit(_where)/select_n | solution.py:124
  81.3 1.1 multiply_add_fusion
  82.9 16.7 %collective-permute-start.1 = (f32[5,4,8,256]{3,2,1,0:T(8,128)S(1)}, f32[5,4,8,256]{3,2,1,0:T(8,128)S(1)}, u32[]{:S(2)}, u32[]{:S(2)}) collective-permute-start(f32[5,4,8,256]{3,2,1,0:T(8,128)S(1)} %get-tuple-element.17), channel_id=1, source_target_pairs={{0,32},{32,0},{64,96},{96,64},{128,160},{160,128},{192,224},{224,1... | collective-permute-start | bytes 491528 | tf_op jit(solution)/shard_map/ppermute | solution.py:29
  99.6 0.8 multiply_dynamic-update-slice_fusion
  100.7 2.1 %collective-permute-start.3 = (f32[5,4,8,256]{3,2,1,0:T(8,128)S(1)}, f32[5,4,8,256]{3,2,1,0:T(8,128)S(1)}, u32[]{:S(2)}, u32[]{:S(2)}) collective-permute-start(f32[5,4,8,256]{3,2,1,0:T(8,128)S(1)} %get-tuple-element.15), channel_id=1, source_target_pairs={{0,96},{32,64},{64,32},{96,0},{128,224},{160,192},{192,160},{224,1... | collective-permute-start | bytes 491528 | tf_op jit(solution)/shard_map/ppermute | solution.py:29
  103.2 2.2 %collective-permute-start.5 = (f32[5,4,8,256]{3,2,1,0:T(8,128)S(1)}, f32[5,4,8,256]{3,2,1,0:T(8,128)S(1)}, u32[]{:S(2)}, u32[]{:S(2)}) collective-permute-start(f32[5,4,8,256]{3,2,1,0:T(8,128)S(1)} %get-tuple-element.13), channel_id=1, source_target_pairs={{0,160},{32,128},{64,224},{96,192},{128,32},{160,0},{192,96},{224,... | collective-permute-start | bytes 491528 | tf_op jit(solution)/shard_map/ppermute | solution.py:29
  105.5 1.0 collective-permute-start.6
  106.5 2.8 %collective-permute-start.7 = (f32[5,4,8,256]{3,2,1,0:T(8,128)S(1)}, f32[5,4,8,256]{3,2,1,0:T(8,128)S(1)}, u32[]{:S(2)}, u32[]{:S(2)}) collective-permute-start(f32[5,4,8,256]{3,2,1,0:T(8,128)S(1)} %get-tuple-element.11), channel_id=1, source_target_pairs={{0,224},{32,192},{64,160},{96,128},{128,96},{160,64},{192,32},{224... | collective-permute-start | bytes 491528 | tf_op jit(solution)/shard_map/ppermute | solution.py:29
  109.3 2.1 %collective-permute-done.3 = f32[5,4,8,256]{3,2,1,0:T(8,128)S(1)} collective-permute-done((f32[5,4,8,256]{3,2,1,0:T(8,128)S(1)}, f32[5,4,8,256]{3,2,1,0:T(8,128)S(1)}, u32[]{:S(2)}, u32[]{:S(2)}) %collective-permute-start.3) | collective-permute-done | bytes 163872 | tf_op jit(solution)/shard_map/ppermute | solution.py:29
  111.4 1.6 %collective-permute-done.4 = f32[5,4,8,256]{3,2,1,0:T(8,128)S(1)} collective-permute-done((f32[5,4,8,256]{3,2,1,0:T(8,128)S(1)}, f32[5,4,8,256]{3,2,1,0:T(8,128)S(1)}, u32[]{:S(2)}, u32[]{:S(2)}) %collective-permute-start.4) | collective-permute-done | bytes 163872 | tf_op jit(solution)/shard_map/ppermute | solution.py:29
  113.1 4.5 %collective-permute-done.5 = f32[5,4,8,256]{3,2,1,0:T(8,128)S(1)} collective-permute-done((f32[5,4,8,256]{3,2,1,0:T(8,128)S(1)}, f32[5,4,8,256]{3,2,1,0:T(8,128)S(1)}, u32[]{:S(2)}, u32[]{:S(2)}) %collective-permute-start.5) | collective-permute-done | bytes 163872 | tf_op jit(solution)/shard_map/ppermute | solution.py:29
  117.6 1.7 %collective-permute-done.6 = f32[5,4,8,256]{3,2,1,0:T(8,128)S(1)} collective-permute-done((f32[5,4,8,256]{3,2,1,0:T(8,128)S(1)}, f32[5,4,8,256]{3,2,1,0:T(8,128)S(1)}, u32[]{:S(2)}, u32[]{:S(2)}) %collective-permute-start.6) | collective-permute-done | bytes 163872 | tf_op jit(solution)/shard_map/ppermute | solution.py:29
  119.3 3.9 %collective-permute-done.7 = f32[5,4,8,256]{3,2,1,0:T(8,128)S(1)} collective-permute-done((f32[5,4,8,256]{3,2,1,0:T(8,128)S(1)}, f32[5,4,8,256]{3,2,1,0:T(8,128)S(1)}, u32[]{:S(2)}, u32[]{:S(2)}) %collective-permute-start.7) | collective-permute-done | bytes 163872 | tf_op jit(solution)/shard_map/ppermute | solution.py:29
  123.9 2.6 %bitcast_add_fusion = f32[5,4,64,256]{3,2,1,0:T(8,128)} fusion(f32[5,4,64,256]{3,2,1,0:T(8,128)} %multiply_dynamic-update-slice_fusion, f32[8,5,4,8,256]{4,3,2,1,0:T(8,128)S(1)} %gather_fusion), kind=kLoop, calls=%fused_computation.30 | loop fusion | flops 327680 | bytes 3932160 | tf_op jit(solution)/shard_map/add | solution.py:183
  (60 shorter events, 5.8 us)
Async XLA Ops:
  0.0 7.5 %copy-start.3 = (f32[5,4,64,256]{3,2,1,0:T(8,128)S(1)}, f32[5,4,64,256]{3,2,1,0:T(8,128)}, u32[]{:S(2)}) copy-start(f32[5,4,64,256]{3,2,1,0:T(8,128)} %param.8) | copy-start | bytes 3932164
  1.2 15.9 %collective-permute-start.8 = (f32[2,4,3,256]{3,2,1,0:T(4,128)S(1)}, f32[2,4,3,256]{3,2,1,0:T(4,128)S(1)}, u32[]{:S(2)}, u32[]{:S(2)}) collective-permute-start(f32[2,4,3,256]{3,2,1,0:T(4,128)S(1)} %get-tuple-element.27), channel_id=1, source_target_pairs={{2,0},{4,2},{6,4},{8,6},{10,8},{12,10},{14,12},{16,14},{18,16},{20... | collective-permute-start | bytes 73736 | tf_op jit(solution)/shard_map/ppermute | solution.py:48
  2.5 14.6 %collective-permute-start.9 = (f32[2,4,3,256]{3,2,1,0:T(4,128)S(1)}, f32[2,4,3,256]{3,2,1,0:T(4,128)S(1)}, u32[]{:S(2)}, u32[]{:S(2)}) collective-permute-start(f32[2,4,3,256]{3,2,1,0:T(4,128)S(1)} %get-tuple-element.28), channel_id=1, source_target_pairs={{0,2},{2,4},{4,6},{6,8},{8,10},{10,12},{12,14},{14,16},{16,18},{18... | collective-permute-start | bytes 73736 | tf_op jit(solution)/shard_map/ppermute | solution.py:45
  9.7 6.4 %copy-start.7 = (f32[4,64]{1,0:T(4,128)S(1)}, f32[4,64]{1,0:T(4,128)}, u32[]{:S(2)}) copy-start(f32[4,64]{1,0:T(4,128)} %param.11) | copy-start | bytes 3076
  9.7 6.5 %copy-start.8 = (f32[4,64]{1,0:T(4,128)S(1)}, f32[4,64]{1,0:T(4,128)}, u32[]{:S(2)}) copy-start(f32[4,64]{1,0:T(4,128)} %param.9) | copy-start | bytes 3076
  9.7 6.5 %copy-start.9 = (f32[4,64]{1,0:T(4,128)S(1)}, f32[4,64]{1,0:T(4,128)}, u32[]{:S(2)}) copy-start(f32[4,64]{1,0:T(4,128)} %param.10) | copy-start | bytes 3076
  9.7 32.8 %all-to-all-start = ((f32[5,4,64,256]{3,0,1,2:T(8,128)}), f32[5,4,64,256]{3,0,1,2:T(8,128)S(1)}, u32[]{:S(2)}, u32[]{:S(2)}) async-start(f32[5,4,64,256]{3,0,1,2:T(8,128)} %copy.31), calls=%async_computation | async-start | bytes 4194304 | tf_op jit(solution)/shard_map/all_to_all | solution.py:168
  17.5 2.2 %copy-start.1 = (f32[2,4,64,256]{3,2,1,0:T(8,128)}, f32[2,4,64,256]{3,2,1,0:T(8,128)S(1)}, u32[]{:S(2)}) copy-start(f32[2,4,64,256]{3,2,1,0:T(8,128)S(1)} %fusion.16) | copy-start | bytes 1572868
  43.2 1.1 copy-start
  46.0 7.7 %copy-start.6 = (f32[128,128,1,1,1]{1,0,4,3,2:T(8,128)S(1)}, f32[128,128,1,1,1]{1,0,4,3,2:T(8,128)}, u32[]{:S(2)}) copy-start(f32[128,128,1,1,1]{1,0,4,3,2:T(8,128)} %constant.82) | copy-start | bytes 196612
  47.6 32.3 %collective-permute-start = (f32[5,3,8,2048]{3,2,1,0:T(8,128)}, f32[5,3,8,2048]{3,2,1,0:T(8,128)}, u32[]{:S(2)}, u32[]{:S(2)}) collective-permute-start(f32[5,3,8,2048]{3,2,1,0:T(8,128)} %fusion.14), channel_id=1, source_target_pairs={{0,1},{1,0},{2,3},{3,2},{4,5},{5,4},{6,7},{7,6},{8,9},{9,8},{10,11... | collective-permute-start | bytes 2949128 | tf_op jit(solution)/shard_map/ppermute | solution.py:37
  54.9 0.8 copy-start.5
  55.8 1.3 %copy-start.4 = (f32[128,128,1,1,1]{1,0,4,3,2:T(8,128)S(1)}, f32[128,128,1,1,1]{1,0,4,3,2:T(8,128)}, u32[]{:S(2)}) copy-start(f32[128,128,1,1,1]{1,0,4,3,2:T(8,128)} %constant.80) | copy-start | bytes 196612
  82.8 16.9 %copy-start.2 = (f32[2,4,64,256]{3,2,1,0:T(8,128)S(1)}, f32[2,4,64,256]{3,2,1,0:T(8,128)}, u32[]{:S(2)}) copy-start(f32[2,4,64,256]{3,2,1,0:T(8,128)} %copy-done.1) | copy-start | bytes 1572868
  82.9 22.5 %collective-permute-start.1 = (f32[5,4,8,256]{3,2,1,0:T(8,128)S(1)}, f32[5,4,8,256]{3,2,1,0:T(8,128)S(1)}, u32[]{:S(2)}, u32[]{:S(2)}) collective-permute-start(f32[5,4,8,256]{3,2,1,0:T(8,128)S(1)} %get-tuple-element.17), channel_id=1, source_target_pairs={{0,32},{32,0},{64,96},{96,64},{128,160},{160,128},{192,224},{224,1... | collective-permute-start | bytes 491528 | tf_op jit(solution)/shard_map/ppermute | solution.py:29
  100.4 6.0 %collective-permute-start.2 = (f32[5,4,8,256]{3,2,1,0:T(8,128)S(1)}, f32[5,4,8,256]{3,2,1,0:T(8,128)S(1)}, u32[]{:S(2)}, u32[]{:S(2)}) collective-permute-start(f32[5,4,8,256]{3,2,1,0:T(8,128)S(1)} %get-tuple-element.16), channel_id=1, source_target_pairs={{0,64},{32,96},{64,0},{96,32},{128,192},{160,224},{192,128},{224,1... | collective-permute-start | bytes 491528 | tf_op jit(solution)/shard_map/ppermute | solution.py:29
  100.7 10.7 %collective-permute-start.3 = (f32[5,4,8,256]{3,2,1,0:T(8,128)S(1)}, f32[5,4,8,256]{3,2,1,0:T(8,128)S(1)}, u32[]{:S(2)}, u32[]{:S(2)}) collective-permute-start(f32[5,4,8,256]{3,2,1,0:T(8,128)S(1)} %get-tuple-element.15), channel_id=1, source_target_pairs={{0,96},{32,64},{64,32},{96,0},{128,224},{160,192},{192,160},{224,1... | collective-permute-start | bytes 491528 | tf_op jit(solution)/shard_map/ppermute | solution.py:29
  102.8 10.2 %collective-permute-start.4 = (f32[5,4,8,256]{3,2,1,0:T(8,128)S(1)}, f32[5,4,8,256]{3,2,1,0:T(8,128)S(1)}, u32[]{:S(2)}, u32[]{:S(2)}) collective-permute-start(f32[5,4,8,256]{3,2,1,0:T(8,128)S(1)} %get-tuple-element.14), channel_id=1, source_target_pairs={{0,128},{32,160},{64,192},{96,224},{128,0},{160,32},{192,64},{224,... | collective-permute-start | bytes 491528 | tf_op jit(solution)/shard_map/ppermute | solution.py:29
  103.2 14.4 %collective-permute-start.5 = (f32[5,4,8,256]{3,2,1,0:T(8,128)S(1)}, f32[5,4,8,256]{3,2,1,0:T(8,128)S(1)}, u32[]{:S(2)}, u32[]{:S(2)}) collective-permute-start(f32[5,4,8,256]{3,2,1,0:T(8,128)S(1)} %get-tuple-element.13), channel_id=1, source_target_pairs={{0,160},{32,128},{64,224},{96,192},{128,32},{160,0},{192,96},{224,... | collective-permute-start | bytes 491528 | tf_op jit(solution)/shard_map/ppermute | solution.py:29
  105.5 13.9 %collective-permute-start.6 = (f32[5,4,8,256]{3,2,1,0:T(8,128)S(1)}, f32[5,4,8,256]{3,2,1,0:T(8,128)S(1)}, u32[]{:S(2)}, u32[]{:S(2)}) collective-permute-start(f32[5,4,8,256]{3,2,1,0:T(8,128)S(1)} %get-tuple-element.12), channel_id=1, source_target_pairs={{0,192},{32,224},{64,128},{96,160},{128,64},{160,96},{192,0},{224,... | collective-permute-start | bytes 491528 | tf_op jit(solution)/shard_map/ppermute | solution.py:29
  106.5 16.8 %collective-permute-start.7 = (f32[5,4,8,256]{3,2,1,0:T(8,128)S(1)}, f32[5,4,8,256]{3,2,1,0:T(8,128)S(1)}, u32[]{:S(2)}, u32[]{:S(2)}) collective-permute-start(f32[5,4,8,256]{3,2,1,0:T(8,128)S(1)} %get-tuple-element.11), channel_id=1, source_target_pairs={{0,224},{32,192},{64,160},{96,128},{128,96},{160,64},{192,32},{224... | collective-permute-start | bytes 491528 | tf_op jit(solution)/shard_map/ppermute | solution.py:29
